TPU v7x, 32 devices: a whole 2x2x4 slice. The times are simulated.
32 devices in a mesh: row: 2 (over x), col: 16 (over z, y, core).
Axes of the slice: x: 2, y: 2, z: 4, core: 2. Of those that a mesh axis runs over, the one named last changes fastest.
Arguments:
- inv_anc: float32 [2, 16, 48, 1536], P(None, 'col', None, 'row'), may hold values from -6 to 6
- factor_cols: float32 [4, 1536, 256], P(None, ('row', 'col')), may hold values from -0.15625 to 0.15625
- couple: float32 [6, 256, 256], replicated, may hold values from -0.1875 to 0.1875
- diag_inv: float32 [4, 256, 256], replicated, may hold values from -6 to 6, as said below
- pattern: int32 [4, 6], replicated, may hold values 0 or 1
- parent: int32 [4], replicated, may hold values from 0 to 4, as said below
Outputs:
- inv_cols: float32 [4, 1536, 256], P(None, ('row', 'col'))
- win_cols: float32 [6, 256, 256], replicated
- win_diag: float32 [4, 256, 256], replicated
Inputs may be any that keep to these rules, and one draw needn't show every extreme that they name: parent[0] is 4, meaning a parent in the ancestor set; for j of 1 or more parent[j] is an earlier supernode or 4. Each diag_inv[j] is symmetric.
All inputs are finite; a program needn't handle non-finite values.
Results may differ from a plain program's by a relative error of at most 0.0001.
Values sent between devices are 32-bit elements; how exact they have to be, the bound alone decides.
A program may use at most 64 MiB of HBM per device.

v0:
```python
import jax
import jax.numpy as jnp
from jax import lax
from jax.sharding import PartitionSpec as P

W = 256
NSUP = 4


exact_mode = lax.Precision.HIGHEST


def product(left, right):
    return jnp.dot(left, right, precision=exact_mode, preferred_element_type=jnp.float32)


def ancestry(parent):
    linked = {}
    for j in range(NSUP):
        for m in range(j):
            linked_now = parent[j] == m
            for p in range(m + 1, j):
                linked_now = linked_now | (parent[j] == p) & linked[p, m]
            linked[j, m] = linked_now
    return linked


def couplings(couple, parent):
    linked = ancestry(parent)
    blocks = {}
    for j in range(NSUP):
        for m in range(j):
            blocks[j, m] = couple[j * (j - 1) // 2 + m] * linked[j, m].astype(jnp.float32)
    return blocks


def window_blocks(crossed, diag_terms, diag_inv, blocks):
    off_diag = {}
    diagonal = []

    def lookup_block(first, second):
        if first == second:
            return diagonal[first]
        if first < second:
            return off_diag[second, first]
        return off_diag[first, second].T

    for j in range(NSUP):
        for m in range(j):
            running = crossed[j, m]
            for q in range(j):
                running = running + product(lookup_block(m, q), blocks[j, q])
            off_diag[j, m] = -running
        diag_value = diag_inv[j] - diag_terms[j]
        for m in range(j):
            diag_value = diag_value - product(blocks[j, m].T, off_diag[j, m])
        diagonal.append(diag_value)
    pair_list = [off_diag[j, m] for j in range(NSUP) for m in range(j)]
    return (jnp.stack(pair_list), jnp.stack(diagonal))


def shards(inv_anc, factor_cols, couple, diag_inv, pattern, parent):
    col_count = lax.axis_size("col")
    local_block = inv_anc.reshape(inv_anc.shape[0] * inv_anc.shape[2], inv_anc.shape[3])
    rows_here = factor_cols.shape[1]
    first_row = (lax.axis_index("row") * col_count + lax.axis_index("col")) * rows_here
    row_ids = first_row + jnp.arange(rows_here, dtype=jnp.int32)
    block_ids = row_ids // W
    one_hot = (block_ids[:, None] == jnp.arange(pattern.shape[1], dtype=jnp.int32)[None, :]).astype(
        jnp.float32
    )
    row_mask = product(one_hot, pattern.astype(jnp.float32).T)
    masked = factor_cols * row_mask.T[:, :, None]
    blocks = couplings(couple, parent)
    reduced = []
    for j in range(NSUP):
        current = masked[j]
        for m in range(j):
            current = current - product(reduced[m], blocks[j, m])
        reduced.append(current)
    joined = jnp.concatenate(reduced, axis=1)
    partial_value = product(local_block, lax.all_gather(joined, "col", axis=0, tiled=True))
    summed = lax.psum_scatter(partial_value, "row", scatter_dimension=0, tiled=True)
    columns = [-summed[:, j * W : (j + 1) * W] for j in range(NSUP)]
    crossed = {}
    diag_terms = []
    for j in range(NSUP):
        products = [product(columns[m].T, masked[j]) for m in range(j)]
        products.append(product(masked[j].T, columns[j]))
        summed_terms = lax.psum(jnp.stack(products), ("row", "col"))
        for m in range(j):
            crossed[j, m] = summed_terms[m]
        diag_terms.append(summed_terms[j])
    pair_blocks, diagonal = window_blocks(crossed, diag_terms, diag_inv, blocks)
    return (jnp.stack(columns), pair_blocks, diagonal)


def solution(mesh):
    in_specs = (P(None, "col", None, "row"), P(None, ("row", "col"), None), P(), P(), P(), P())
    out_specs = (P(None, ("row", "col"), None), P(), P())
    return jax.shard_map(shards, mesh=mesh, in_specs=in_specs, out_specs=out_specs, check_vma=False)
```

profile of v0, /device:TPU:0, one launch (start us, length us, event | category | flops | bytes accessed | tf_op | source)
XLA Modules:
  0.0 250.8 jit_solution(1769660225671560775)
XLA Ops:
  7.2 1.4 fusion.71
  12.6 0.9 convolution_bitcast_fusion.11
  13.5 1.0 broadcast_multiply_fusion
  14.5 1.2 convolution_subtract_fusion.11
  15.7 1.2 convolution_subtract_fusion.8
  16.9 1.2 convolution_subtract_fusion.10
  18.9 0.7 pad_maximum_fusion.4
  19.7 48.0 %all-gather.2.cloned.1.call-done = f32[768,1024]{1,0:T(8,128)} async-done(((f32[48,1024]{1,0:T(8,128)}), f32[768,1024]{1,0:T(8,128)}) %all-gather.2.cloned.1.call-update) | async-done | bytes 3145744 | tf_op jit(solution)/shard_map/all_gather | solution.py:82
  67.7 4.6 %convolution_bitcast_fusion = f32[96,1024]{1,0:T(8,128)} fusion(f32[768,1024]{1,0:T(8,128)} %all-gather.2.cloned.1.call-done, f32[96,768]{1,0:T(8,128)S(1)} %bitcast.219), kind=kOutput, calls=%fused_computation | convolution fusion | flops 905969664 | bytes 3833856 | tf_op jit(solution)/shard_map/dot_general | solution.py:14
  72.6 11.8 %reduce-scatter.2.cloned.1.call-done = f32[48,1024]{1,0:T(8,128)} async-done(((f32[96,1024]{1,0:T(8,128)}), f32[48,1024]{1,0:T(8,128)}) %reduce-scatter.2.cloned.1.call-update) | async-done | bytes 196624 | tf_op jit(solution)/shard_map/reduce_scatter | solution.py:83
  84.4 1.3 convolution_bitcast_fusion.9
  85.7 1.2 convolution_bitcast_fusion.10
  86.9 0.8 pad_maximum_fusion.3
  87.8 0.4 convolution_bitcast_fusion.6
  89.0 0.9 pad_maximum_fusion.2
  91.7 1.1 pad_maximum_fusion
  92.7 1.1 convolution_bitcast_fusion.8
  93.9 0.7 pad_maximum_fusion.5
  94.6 136.5 %all-reduce.3.cloned.1.call-done = (f32[2,256,256]{2,1,0:T(8,128)}, f32[1,256,256]{2,1,0:T(8,128)}, f32[3,256,256]{2,1,0:T(8,128)}, f32[4,256,256]{2,1,0:T(8,128)}) async-done(((f32[2,256,256]{2,1,0:T(8,128)}, f32[1,256,256]{2,1,0:T(8,128)}, f32[3,256,256]{2,1,0:T(8,128)}, f32[4,256,256]{2,1,0:T(8,128)}), (f32[2,256,256]{2,1,0:T(8,128)}, f32[1,256,256]{2,1,0:T(8,128)}, f32[3,256,256]{2,1,0:T(8,128)}, ...) | async-done | bytes 2621456 | tf_op jit(solution)/shard_map/psum | solution.py:90
  231.1 1.1 slice_subtract_fusion.3
  232.2 1.3 convolution_add_fusion.12
  234.3 0.6 convolution_subtract_fusion.5
  235.3 0.6 convolution_add_fusion.2
  236.0 0.6 convolution_subtract_fusion.4
  236.6 0.6 convolution_add_fusion.10
  237.2 0.6 convolution_add_fusion.5
  239.4 0.6 convolution_subtract_fusion.2
  240.0 0.6 convolution_subtract_fusion.3
  240.6 0.6 convolution_add_fusion.1
  241.6 0.6 convolution_subtract_fusion.1
  242.6 0.6 fusion
  243.2 1.0 pad_maximum_fusion.1
  (43 shorter events, 7.2 us)
Async XLA Ops:
  7.2 60.5 %copy-start = (f32[2,1,48,768]{3,2,1,0:T(8,128)S(1)}, f32[2,1,48,768]{3,2,1,0:T(8,128)}, u32[]{:S(2)}) copy-start(f32[2,1,48,768]{3,2,1,0:T(8,128)} %param.6) | copy-start | bytes 884740
  7.2 11.0 %copy-start.1 = (f32[6,256,256]{2,1,0:T(8,128)S(1)}, f32[6,256,256]{2,1,0:T(8,128)}, u32[]{:S(2)}) copy-start(f32[6,256,256]{2,1,0:T(8,128)} %param.8) | copy-start | bytes 4718596
  7.2 60.5 %all-gather.2.cloned.1.call-start = ((), (), s32[]{:S(2)}) async-start(), calls=%async_computation.1 | async-start | bytes 3342336 | tf_op jit(solution)/shard_map/all_gather | solution.py:82
  19.7 64.8 %reduce-scatter.2.cloned.1.call-start = ((), (), s32[]{:S(2)}) async-start(), calls=%async_computation.2 | async-start | bytes 589824 | tf_op jit(solution)/shard_map/reduce_scatter | solution.py:83
  72.4 158.7 %all-reduce.3.cloned.1.call-start = ((), (), s32[]{:S(2)}) async-start(), calls=%async_computation.3 | async-start | bytes 5242880 | tf_op jit(solution)/shard_map/psum | solution.py:90
  84.4 3.3 %copy-start.2 = (f32[48,1024]{1,0:T(8,128)S(1)}, f32[48,1024]{1,0:T(8,128)}, u32[]{:S(2)}) copy-start(f32[48,1024]{1,0:T(8,128)} %reduce-scatter.2.cloned.1.call-done) | copy-start | bytes 589828
  93.8 137.2 %copy-start.3 = (f32[4,256,256]{2,1,0:T(8,128)S(1)}, f32[4,256,256]{2,1,0:T(8,128)}, u32[]{:S(2)}) copy-start(f32[4,256,256]{2,1,0:T(8,128)} %param.9) | copy-start | bytes 3145732
  231.1 2.5 copy-start.4
  231.1 2.9 %copy-start.6 = (f32[2,256,256]{2,1,0:T(8,128)S(1)}, f32[2,256,256]{2,1,0:T(8,128)}, u32[]{:S(2)}) copy-start(f32[2,256,256]{2,1,0:T(8,128)} %get-tuple-element.3) | copy-start | bytes 1572868
  234.3 1.6 copy-start.5
  242.6 1.7 copy-start.7
Sparse Core Ops, SparseCore 0:
  19.8 47.8 all-gather.1
  72.5 11.9 reduce-scatter.1
  94.0 137.0 all-reduce.2
where the time goes:
time: 251 us
  waiting for transfers between devices  196 us (78%)
  matrix products  27.2 us (11%)
  between operations  18.1 us (7%)
  other arithmetic  7.43 us (3%)
    psum x1, waiting for transfers between devices, shards(): summed_terms = lax.psum(jnp.stack(products), ('row', 'col'))  136 us
    all_gather x1, waiting for transfers between devices, shards(): lax.all_gather(joined, 'col', axis=0, tiled=True)  48 us
    dot_general x38, matrix products, product(): jnp.dot(left, right, precision=exact_mode, preferred_element_type=jnp.flo...  27.2 us
    reduce_scatter x1, waiting for transfers between devices, shards(): lax.psum_scatter(partial_value, 'row', scatter_dimension=0, tiled=True)  11.8 us
  transfers between devices with their start and end apart: 3, of which 3 were waited for; matrix products, arithmetic and copies ran while one was open for 0% of the time, Pallas kernels for 0%

commit v1 on v0

v1 whole, which is shorter than its diff:
```python
import jax
import jax.numpy as jnp
from jax import lax
from jax.sharding import PartitionSpec as P


def product(left, right):
    return jnp.dot(
        left, right, precision=lax.Precision.HIGH, preferred_element_type=jnp.float32
    )


def ancestry(parent):
    linked = {}
    for j in range(parent.shape[0]):
        for m in range(j):
            linked_now = parent[j] == m
            for p in range(m + 1, j):
                linked_now = linked_now | (parent[j] == p) & linked[p, m]
            linked[j, m] = linked_now
    return linked


def couplings(couple, parent):
    linked = ancestry(parent)
    return {
        (j, m): couple[j * (j - 1) // 2 + m] * linked[j, m].astype(jnp.float32)
        for j, m in linked
    }


def inverse_coupling(blocks, count, width):
    inverse = {}
    for m in range(count):
        inverse[m, m] = jnp.eye(width, dtype=jnp.float32)
        for j in range(m + 1, count):
            total = blocks[j, m]
            for q in range(m + 1, j):
                total = total + product(inverse[m, q], blocks[j, q])
            inverse[m, j] = -total
    return inverse


def shards(inv_anc, factor_cols, couple, diag_inv, pattern, parent):
    count, rows_here, width = factor_cols.shape
    col_count, row_count = lax.axis_size("col"), lax.axis_size("row")
    total_width = count * width
    local_block = inv_anc.reshape(inv_anc.shape[0] * inv_anc.shape[2], inv_anc.shape[3])
    first_row = (lax.axis_index("row") * col_count + lax.axis_index("col")) * rows_here
    block_ids = (first_row + jnp.arange(rows_here, dtype=jnp.int32)) // width
    row_mask = jnp.take(pattern, block_ids, axis=1).astype(jnp.float32)
    masked = factor_cols * row_mask[:, :, None]
    blocks = couplings(couple, parent)
    reduced = []
    for j in range(count):
        current = masked[j]
        for m in range(j):
            current = current - product(reduced[m], blocks[j, m])
        reduced.append(current)
    joined = jnp.concatenate(reduced, axis=1)
    gathered = lax.all_gather(joined, "col", axis=0, tiled=True)
    partial_value = product(local_block, gathered)
    summed = lax.psum_scatter(partial_value, "row", scatter_dimension=0, tiled=True)
    columns = jnp.stack([-summed[:, j * width : (j + 1) * width] for j in range(count)])
    inverse = inverse_coupling(blocks, count, width)
    zero = jnp.zeros((width, width), jnp.float32)
    whole = jnp.concatenate(
        [
            jnp.concatenate([inverse.get((m, j), zero) for j in range(count)], axis=1)
            for m in range(count)
        ],
        axis=0,
    )
    slab = total_width // col_count
    own = lax.dynamic_slice_in_dim(whole, lax.axis_index("col") * slab, slab, axis=1)
    weighted = jnp.concatenate(
        [product(own[q * width : (q + 1) * width].T, diag_inv[q]) for q in range(count)],
        axis=1,
    )
    window = product(weighted, whole)
    exchanged = lax.all_to_all(summed, "col", split_axis=1, concat_axis=0, tiled=True)
    slab_rows = lax.psum_scatter(
        product(exchanged.T, gathered), "row", scatter_dimension=0, tiled=True
    )
    part = slab // row_count
    slab_rows = slab_rows + lax.dynamic_slice_in_dim(
        window, lax.axis_index("row") * part, part, axis=0
    )
    full = lax.all_gather(slab_rows, ("col", "row"), axis=0, tiled=True)

    def block(m, j):
        return full[m * width : (m + 1) * width, j * width : (j + 1) * width]

    pairs = jnp.stack([block(m, j) for j in range(count) for m in range(j)])
    diagonal = jnp.stack([block(j, j) for j in range(count)])
    return columns, pairs, diagonal


def solution(mesh):
    in_specs = (P(None, "col", None, "row"), P(None, ("row", "col"), None), P(), P(), P(), P())
    out_specs = (P(None, ("row", "col"), None), P(), P())
    return jax.shard_map(shards, mesh=mesh, in_specs=in_specs, out_specs=out_specs, check_vma=False)
```

time: 251 us -> 202 us (0.80)
  waiting for transfers between devices: 196 us -> 120 us
  local copies, waits for them, and re-layouts: 1.45 us -> 23.9 us
  matrix products: 27.2 us -> 21 us
  starting transfers between devices: 0.3 us -> 5.84 us
  other arithmetic: 7.43 us -> 12.5 us
    psum x1 -> x0, waiting for transfers between devices: 136 us -> none  [shards(): summed_terms = lax.psum(jnp.stack(products), ('row', 'col'))]
    all_gather x1 -> x2, waiting for transfers between devices: 48 us -> 106 us  [the longest x1 63.2 us: shards(): full = lax.all_gather(slab_rows, ('col', 'row'), axis=0, tiled=True)]
    unnamed x16 -> x30, local copies, waits for them, and re-layouts: 0.04 us -> 13.9 us
    reduce_scatter x1, waiting for transfers between devices: 11.8 us -> 4.9 us  [shards(): lax.psum_scatter(partial_value, 'row', scatter_dimension=0, tiled=True)]
    dot_general x38 -> x17, matrix products: 27.2 us -> 21 us  [product(): jnp.dot(left, right, precision=lax.Precision.HIGH, preferred_element_type...]
    all_to_all x0 -> x1, starting transfers between devices: none -> 5.68 us  [shards(): lax.all_to_all(summed, 'col', split_axis=1, concat_axis=0, tiled=True)]
    all_to_all x0 -> x1, waiting for transfers between devices: none -> 5.34 us  [shards(): lax.all_to_all(summed, 'col', split_axis=1, concat_axis=0, tiled=True)]
    all_to_all x0 -> x3, local copies, waits for them, and re-layouts: none -> 4.17 us  [shards(): lax.all_to_all(summed, 'col', split_axis=1, concat_axis=0, tiled=True)]
  transfers between devices with their start and end apart: 3 -> 5, of which waited for: 3 -> 5; matrix products, arithmetic and copies ran while one was open for 0% -> 10% of each run, Pallas kernels for 0% -> 0%
where the time goes in v1:
time: 202 us; the launch traced here: 201 us
  waiting for transfers between devices  120 us (59%)
  local copies, waits for them, and re-layouts  23.9 us (12%)
  matrix products  21 us (10%)
  between operations  18 us (9%)
  other arithmetic  12.5 us (6%)
  starting transfers between devices  5.84 us (3%)
    all_gather x1, waiting for transfers between devices, shards(): full = lax.all_gather(slab_rows, ('col', 'row'), axis=0, tiled=True)  63.2 us
    all_gather x1, waiting for transfers between devices, shards(): gathered = lax.all_gather(joined, 'col', axis=0, tiled=True)  43.1 us
    dot_general x17, matrix products, product(): jnp.dot(left, right, precision=lax.Precision.HIGH, preferred_element_type...  21 us
    unnamed x30, local copies, waits for them, and re-layouts  13.9 us
    all_to_all x1, starting transfers between devices, shards(): lax.all_to_all(summed, 'col', split_axis=1, concat_axis=0, tiled=True)  5.68 us
    all_to_all x1, waiting for transfers between devices, shards(): lax.all_to_all(summed, 'col', split_axis=1, concat_axis=0, tiled=True)  5.34 us
    reduce_scatter x1, waiting for transfers between devices, shards(): lax.psum_scatter(partial_value, 'row', scatter_dimension=0, tiled=True)  4.9 us
    all_to_all x3, local copies, waits for them, and re-layouts, shards(): lax.all_to_all(summed, 'col', split_axis=1, concat_axis=0, tiled=True)  4.17 us
  transfers between devices with their start and end apart: 5, of which 5 were waited for; matrix products, arithmetic and copies ran while one was open for 10% of the time, Pallas kernels for 0%

profile of v1, /device:TPU:0, one launch (start us, length us, event | category | flops | bytes accessed | tf_op | source)
XLA Modules:
  0.0 201.0 jit_solution(15975654702477398432)
XLA Ops:
  7.2 1.4 fusion.76
  12.6 1.5 fusion.75
  20.6 1.0 fusion
  22.8 1.0 fusion.1
  23.8 43.1 %all-gather.3.cloned.1.call-done = f32[768,1024]{1,0:T(8,128)} async-done(((f32[48,1024]{1,0:T(8,128)}), f32[768,1024]{1,0:T(8,128)}) %all-gather.3.cloned.1.call-update) | async-done | bytes 3145744 | tf_op jit(solution)/shard_map/all_gather | solution.py:61
  66.9 3.6 %convolution_bitcast_fusion = f32[96,1024]{1,0:T(8,128)} fusion(f32[768,1024]{1,0:T(8,128)} %all-gather.3.cloned.1.call-done, f32[96,768]{1,0:T(8,128)S(1)} %bitcast.136), kind=kOutput, calls=%fused_computation.3 | convolution fusion | flops 452984832 | bytes 3833856 | tf_op jit(solution)/shard_map/dot_general | solution.py:8
  70.6 4.0 %select_maximum_fusion = f32[1024,1024]{0,1:T(8,128)S(1)} fusion(f32[256,256]{0,1:T(8,128)} %fusion.41, f32[256,256]{0,1:T(8,128)} %get-tuple-element.20, f32[256,512]{0,1:T(8,128)S(1)} %concatenate.28, f32[256,256]{0,1:T(8,128)} %fusion, f32[256,256]{0,1:T(8,128)} %get-tuple-element.21, f32[256,256]{0,1:T(8,128)S(1)} %broadcast_in_dim.16, ...), kind=kLoop, calls=%fused_computation.1 | loop fusion | flops 13631488 | bytes 6815744 | tf_op jit(solution)/shard_map/concatenate | solution.py:67
  74.6 1.9 copy-done.1
  76.6 1.2 fusion.23
  77.7 4.9 %reduce-scatter.3.cloned.1.call-done = f32[48,1024]{1,0:T(8,128)} async-done(((f32[96,1024]{1,0:T(8,128)}), f32[48,1024]{1,0:T(8,128)}) %reduce-scatter.3.cloned.1.call-update) | async-done | bytes 196624 | tf_op jit(solution)/shard_map/reduce_scatter | solution.py:63
  82.6 1.8 all_to_all.14
  84.4 1.9 copy.44
  86.3 1.9 reshape.134
  88.2 5.7 %all-to-all-start = ((f32[16,1,3072]{2,1,0:T(1,128)}), f32[16,1,3072]{2,1,0:T(1,128)}, u32[]{:S(2)}, u32[]{:S(2)}) async-start(f32[16,1,3072]{2,1,0:T(1,128)} %reshape.134), calls=%async_computation.1 | async-start | bytes 393216 | tf_op jit(solution)/shard_map/all_to_all | solution.py:81
  93.9 1.8 fusion.17
  95.8 1.8 fusion.19
  97.6 5.3 %all-to-all-done = f32[16,1,3072]{2,1,0:T(1,128)} async-done(((f32[16,1,3072]{2,1,0:T(1,128)}), f32[16,1,3072]{2,1,0:T(1,128)}, u32[]{:S(2)}, u32[]{:S(2)}) %all-to-all-start) | async-done | bytes 196640 | tf_op jit(solution)/shard_map/all_to_all | solution.py:81
  103.4 2.7 %reduce = f32[16,3072]{1,0:T(8,128)} reduce(f32[16,1,3072]{2,1,0:T(1,128)} %all-to-all-done, f32[]{:T(128)} %broadcast.158), dimensions={1}, to_apply=%all_to_all.15.reduce_sub_computation | reduce | bytes 393220 | tf_op jit(solution)/shard_map/all_to_all | solution.py:81
  106.2 1.8 reshape.135
  108.0 2.8 %fusion.77 = f32[64,1024]{1,0:T(8,128)} fusion(f32[768,64]{1,0:T(8,128)} %bitcast.137, f32[768,1024]{1,0:T(8,128)S(1)} %copy-done.2), kind=kOutput, calls=%fused_computation.132 | convolution fusion | flops 301989888 | bytes 3604480 | tf_op jit(solution)/shard_map/dot_general | solution.py:8
  110.8 1.2 fusion.21
  112.1 4.4 %fusion.9 = f32[64,1024]{1,0:T(8,128)S(1)} fusion(f32[1024,1024]{0,1:T(8,128)} %copy-done.1, f32[64,256]{1,0:T(8,128)} %fusion.17, f32[64,256]{1,0:T(8,128)} %fusion.19, f32[64,256]{1,0:T(8,128)S(1)} %fusion.21, f32[64,256]{1,0:T(8,128)S(1)} %fusion.23), kind=kOutput, calls=%fused_computation.34 | convolution fusion | flops 402849792 | bytes 4718592 | tf_op jit(solution)/shard_map/dot_general | solution.py:8
  116.5 3.2 %reduce-scatter.5.cloned.1.call-done = f32[32,1024]{1,0:T(8,128)} async-done(((f32[64,1024]{1,0:T(8,128)}), f32[32,1024]{1,0:T(8,128)}) %reduce-scatter.5.cloned.1.call-update) | async-done | bytes 131088 | tf_op jit(solution)/shard_map/reduce_scatter | solution.py:82
  119.6 1.6 dynamic-slice_add_fusion
  121.9 63.2 %all-gather.5.cloned.1.call-done = f32[1024,1024]{1,0:T(8,128)} async-done(((f32[32,1024]{1,0:T(8,128)}), f32[1024,1024]{1,0:T(8,128)}) %all-gather.5.cloned.1.call-update) | async-done | bytes 4194320 | tf_op jit(solution)/shard_map/all_gather | solution.py:89
  185.2 1.3 slice_bitcast_fusion.3
  186.5 1.0 pad_maximum_fusion
  188.5 1.0 fusion.7
  189.4 1.0 fusion.6
  190.4 1.0 fusion.5
  191.4 1.0 fusion.4
  193.3 1.1 copy-done.7
  (56 shorter events, 11.1 us)
Async XLA Ops:
  7.2 59.8 %copy-start = (f32[2,1,48,768]{3,2,1,0:T(8,128)S(1)}, f32[2,1,48,768]{3,2,1,0:T(8,128)}, u32[]{:S(2)}) copy-start(f32[2,1,48,768]{3,2,1,0:T(8,128)} %param.6) | copy-start | bytes 884740
  7.2 9.2 %copy-start.6 = (f32[4,48,256]{2,1,0:T(8,128)S(1)}, f32[4,48,256]{2,1,0:T(8,128)}, u32[]{:S(2)}) copy-start(f32[4,48,256]{2,1,0:T(8,128)} %param.7) | copy-start | bytes 589828
  7.2 59.7 %all-gather.3.cloned.1.call-start = ((), (), s32[]{:S(2)}) async-start(), calls=%async_computation.3 | async-start | bytes 3342336 | tf_op jit(solution)/shard_map/all_gather | solution.py:61
  18.9 63.7 %reduce-scatter.3.cloned.1.call-start = ((), (), s32[]{:S(2)}) async-start(), calls=%async_computation.4 | async-start | bytes 589824 | tf_op jit(solution)/shard_map/reduce_scatter | solution.py:63
  19.7 2.4 %copy-start.3 = (f32[256,256]{0,1:T(8,128)}, f32[256,256]{0,1:T(8,128)S(1)}, u32[]{:S(2)}) copy-start(f32[256,256]{0,1:T(8,128)S(1)} %negate_bitcast_fusion) | copy-start | bytes 786436
  22.1 0.7 copy-start.4
  70.6 37.3 %copy-start.2 = (f32[768,1024]{1,0:T(8,128)S(1)}, f32[768,1024]{1,0:T(8,128)}, u32[]{:S(2)}) copy-start(f32[768,1024]{1,0:T(8,128)} %all-gather.3.cloned.1.call-done) | copy-start | bytes 9437188
  74.6 2.0 copy-start.1
  88.2 14.7 %all-to-all-start = ((f32[16,1,3072]{2,1,0:T(1,128)}), f32[16,1,3072]{2,1,0:T(1,128)}, u32[]{:S(2)}, u32[]{:S(2)}) async-start(f32[16,1,3072]{2,1,0:T(1,128)} %reshape.134), calls=%async_computation.1 | async-start | bytes 393216 | tf_op jit(solution)/shard_map/all_to_all | solution.py:81
  93.9 25.7 %reduce-scatter.5.cloned.1.call-start = ((), (), s32[]{:S(2)}) async-start(), calls=%async_computation.5 | async-start | bytes 393216 | tf_op jit(solution)/shard_map/reduce_scatter | solution.py:82
  110.8 10.5 %copy-start.5 = (f32[48,1024]{1,0:T(8,128)S(1)}, f32[48,1024]{1,0:T(8,128)}, u32[]{:S(2)}) copy-start(f32[48,1024]{1,0:T(8,128)} %reduce-scatter.3.cloned.1.call-done) | copy-start | bytes 589828
  110.8 74.4 %all-gather.5.cloned.1.call-start = ((), (), s32[]{:S(2)}) async-start(), calls=%async_computation.6 | async-start | bytes 4325376 | tf_op jit(solution)/shard_map/all_gather | solution.py:89
  193.3 1.1 copy-start.7
Sparse Core Ops, SparseCore 0:
  19.0 47.8 all-gather.2
  70.7 11.9 reduce-scatter.2
  110.9 8.6 reduce-scatter.4
  123.0 62.0 all-gather.4

commit v2 on v1

--- a/solution.py
+++ b/solution.py
@@ -1,7 +1,13 @@
+import functools
+
 import jax
 import jax.numpy as jnp
 from jax import lax
+from jax.experimental import pallas as pl
+from jax.experimental.pallas import tpu as pltpu
 from jax.sharding import PartitionSpec as P
+
+MESH = pl.DeviceIdType.MESH
 
 
 def product(left, right):
@@ -96,7 +102,336 @@
     return columns, pairs, diagonal
 
 
+def split(value):
+    high = value.astype(jnp.bfloat16)
+    return high, (value - high.astype(jnp.float32)).astype(jnp.bfloat16)
+
+
+def dot3(left, right):
+    (a, b), (c, d) = left, right
+    return (
+        jnp.dot(a, c, preferred_element_type=jnp.float32)
+        + jnp.dot(a, d, preferred_element_type=jnp.float32)
+        + jnp.dot(b, c, preferred_element_type=jnp.float32)
+    )
+
+
+def window_kernel(
+    n_col, pattern, parent, anc, factor, couple, diag, cols_out, win_out,
+    links, inverse, gath, ypart, xbuf, yown, ysl, gpart, gbuf,
+    z_s, z_r, y_s, y_r, k_s, k_r, x_s, x_r, a_s, a_r, b_s, b_r, g_s, g_r,
+    fz_s, fz_r, fp_s, fp_r, fq_s, fq_r, fk_s, fk_r,
+):
+    count, rows, width = factor.shape
+    n_z, n_chip, slab = n_col // 4, n_col // 2, ysl.shape[1]
+    halves = width // slab
+    npair = couple.shape[0]
+    r, c = lax.axis_index("row"), lax.axis_index("col")
+    core, chip = c % 2, c // 2
+    y, z = chip % 2, chip // 2
+
+    def col_of(zz, yy, kk):
+        return (zz * 2 + yy) * 2 + kk
+
+    def behind(d):
+        return (z + n_z - d) % n_z
+
+    barrier = pltpu.get_barrier_semaphore()
+    for e in range(1, n_col):
+        pl.semaphore_signal(barrier, inc=1, device_id=(r, (c + e) % n_col), device_id_type=MESH)
+    pl.semaphore_signal(barrier, inc=1, device_id=(1 - r, c), device_id_type=MESH)
+
+    def remote(src, dst, send, recv, device):
+        return pltpu.make_async_remote_copy(
+            src_ref=src, dst_ref=dst, send_sem=send, recv_sem=recv,
+            device_id=device, device_id_type=MESH,
+        )
+
+    y_dev, k_dev, x_dev = (r, col_of(z, 1 - y, core)), (r, col_of(z, y, 1 - core)), (1 - r, c)
+    ended = []
+
+    def begin(copy):
+        copy.start()
+        ended.append(copy)
+
+    def slot(j, index):
+        return gath.at[j, pl.ds(pl.multiple_of(index * rows, 16), rows), :]
+
+    linked = {}
+    for j in range(count):
+        for m in range(j):
+            now = parent[j] == m
+            for p in range(m + 1, j):
+                now = jnp.logical_or(now, jnp.logical_and(parent[j] == p, linked[p, m]))
+            linked[j, m] = now
+            pair = j * (j - 1) // 2 + m
+            links[pair] = couple[pair] * jnp.where(now, 1.0, 0.0)
+    first_row = (r * n_col + c) * rows
+    first_block, last_block = first_row // width, (first_row + rows - 1) // width
+    inside = lax.broadcasted_iota(jnp.int32, (rows, width), 0) < (first_block + 1) * width - first_row
+
+    reduced = []
+    for j in range(count):
+        mask = jnp.where(
+            inside,
+            pattern[j, first_block].astype(jnp.float32),
+            pattern[j, last_block].astype(jnp.float32),
+        )
+        current = factor[j] * mask
+        for m in range(j):
+            current = current - dot3(reduced[m], split(links[j * (j - 1) // 2 + m]))
+        reduced.append(split(current))
+        gath[j, pl.ds(pl.multiple_of(c * rows, 16), rows), :] = current
+        if j == 0:
+            pl.semaphore_wait(barrier, n_col)
+        own = slot(j, c)
+        begin(remote(own, own, y_s.at[j, 0], y_r.at[j, 0], y_dev))
+        for d in range(1, n_z):
+            there = (r, col_of((z + d) % n_z, y, core))
+            begin(remote(own, own, z_s.at[j, d], z_r.at[j, d], there))
+        begin(remote(own, own, k_s.at[j, 0], k_r.at[j, 0], k_dev))
+
+    diagonal = (
+        lax.broadcasted_iota(jnp.int32, (width, width), 0)
+        == lax.broadcasted_iota(jnp.int32, (width, width), 1)
+    )
+    for m in range(count):
+        inverse[m, m] = jnp.where(diagonal, 1.0, 0.0)
+        for j in range(m):
+            inverse[m, j] = jnp.zeros((width, width), jnp.float32)
+        for j in range(m + 1, count):
+            total = links[j * (j - 1) // 2 + m]
+            for q in range(m + 1, j):
+                total = total + dot3(split(inverse[m, q]), split(links[j * (j - 1) // 2 + q]))
+            inverse[m, j] = -total
+
+    for j in range(count):
+        for d in range(1, n_z):
+            piece = slot(j, col_of(behind(d), y, core))
+            remote(piece, piece, z_s.at[j, d], z_r.at[j, d], y_dev).wait_recv()
+            begin(remote(piece, piece, y_s.at[j, d], y_r.at[j, d], y_dev))
+            begin(remote(piece, piece, k_s.at[j, d], k_r.at[j, d], k_dev))
+
+    m, h = chip // halves, chip % halves
+
+    def q_of(rr):
+        rho = (rr + z) % 2
+        return (1 - core) * 3 * rho + core * (2 - rho)
+
+    q_own, q_other = q_of(r), q_of(1 - r)
+    j_own, j_other = jnp.minimum(m + q_own, count - 1), jnp.minimum(m + q_other, count - 1)
+    half = pl.ds(pl.multiple_of(h * slab, slab), slab)
+    piece_sum = jnp.zeros((slab, width), jnp.float32)
+    for q in range(count):
+        left = inverse[q, m, :, half].T
+        middle = dot3(split(left), split(diag[q]))
+        piece_sum = piece_sum + dot3(split(middle), split(inverse[q, j_own]))
+    gpart[2] = piece_sum
+
+    left_anc = split(anc[...].reshape(2 * rows, anc.shape[2]))
+
+    def relay(j):
+        for d in range(n_z):
+            piece = slot(j, col_of(behind(d), 1 - y, core))
+            remote(piece, piece, y_s.at[j, d], y_r.at[j, d], y_dev).wait_recv()
+            begin(remote(piece, piece, k_s.at[j, n_z + d], k_r.at[j, n_z + d], k_dev))
+
+    def multiply(j):
+        for d in range(n_z):
+            for side, yy in ((0, y), (1, 1 - y)):
+                piece = slot(j, col_of(behind(d), yy, 1 - core))
+                at = side * n_z + d
+                remote(piece, piece, k_s.at[j, at], k_r.at[j, at], k_dev).wait_recv()
+        ypart[j] = dot3(left_anc, split(gath[j])).reshape(2, rows, width)
+        begin(remote(ypart.at[j, 1 - r], xbuf.at[j], x_s.at[j], x_r.at[j], x_dev))
+
+    def scatter(j):
+        remote(ypart.at[j, 1 - r], xbuf.at[j], x_s.at[j], x_r.at[j], x_dev).wait_recv()
+        total = ypart[j, r] + xbuf[j]
+        yown[j] = total
+        cols_out[j] = -total
+        for part in range(halves):
+            s = j * halves + part
+            src = yown.at[j, :, pl.ds(part * slab, slab)]
+            dst = ysl.at[pl.ds(pl.multiple_of(c * rows, 16), rows), :]
+
+            @pl.when(chip == s)
+            def _():
+                ysl[pl.ds(pl.multiple_of(c * rows, 16), rows), :] = total[:, part * slab : (part + 1) * slab]
+
+            @pl.when(chip != s)
+            def _():
+                remote(src, dst, a_s.at[s], a_r.at[chip], (r, 2 * s + core)).start()
+
+    for j in range(count):
+        relay(j)
+        if j > 0:
+            multiply(j - 1)
+        if j > 1:
+            scatter(j - 2)
+    multiply(count - 1)
+    scatter(count - 2)
+    scatter(count - 1)
+
+    def slab_rows(index):
+        return ysl.at[pl.ds(pl.multiple_of(index * rows, 16), rows), :]
+
+    for e in range(n_chip):
+        other = (chip + n_chip - e) % n_chip
+        piece = slab_rows(2 * other + core)
+        if e:
+            remote(piece, piece, a_s.at[0], a_r.at[other], k_dev).wait_recv()
+        begin(remote(piece, piece, b_s.at[e], b_r.at[e], k_dev))
+    for e in range(n_chip):
+        other = (chip + n_chip - e) % n_chip
+        piece = slab_rows(2 * other + 1 - core)
+        remote(piece, piece, b_s.at[e], b_r.at[e], k_dev).wait_recv()
+    left = split(ysl[...].T)
+    gpart[1] = dot3(left, split(gath[j_other]))
+    begin(remote(gpart.at[1], gbuf, g_s, g_r, x_dev))
+    gpart[0] = dot3(left, split(gath[j_own])) + gpart[2]
+    remote(gpart.at[1], gbuf, g_s, g_r, x_dev).wait_recv()
+
+    def place(rr, zz, yy, kk):
+        rho = (rr + zz) % 2
+        q = (1 - kk) * 3 * rho + kk * (2 - rho)
+        block, part = (2 * zz + yy) // halves, (2 * zz + yy) % halves
+        j = block + q
+        off = (q + 3) // 4
+        index = off * (j * (j - 1) // 2 + block) + (1 - off) * (npair + block)
+        return j < count, index * 1, part
+
+    def at_piece(where):
+        _, index, part = where
+        return win_out.at[index, pl.ds(pl.multiple_of(part * slab, slab), slab), :]
+
+    flip_y, flip_x = 1 - 2 * y, 1 - 2 * r
+    r1, y1 = r + core * flip_x, y + (1 - core) * flip_y
+    r2, y2 = r + (1 - core) * flip_x, y + core * flip_y
+    p_dev, q_dev = (r1, col_of(z, y1, core)), (r2, col_of(z, y2, core))
+    late = []
+
+    def later(needed, copy):
+        @pl.when(needed)
+        def _():
+            copy().start()
+
+        late.append((needed, copy))
+
+    def send(where, send_sem, recv_sem, device):
+        def copy():
+            piece = at_piece(where)
+            return remote(piece, piece, send_sem, recv_sem, device)
+
+        later(where[0], copy)
+
+    def receive(where, send_sem, recv_sem, device):
+        @pl.when(where[0])
+        def _():
+            piece = at_piece(where)
+            remote(piece, piece, send_sem, recv_sem, device).wait_recv()
+
+    mine = place(r, z, y, core)
+
+    @pl.when(mine[0])
+    def _():
+        win_out[mine[1], pl.ds(pl.multiple_of(mine[2] * slab, slab), slab), :] = gpart[0] + gbuf[...]
+
+    for d in range(1, n_z):
+        send(mine, fz_s.at[d], fz_r.at[d], (r, col_of((z + d) % n_z, y, core)))
+    for d in range(n_z):
+        where = place(r, behind(d), y, core)
+        if d:
+            receive(where, fz_s.at[d], fz_r.at[d], k_dev)
+        send(where, fp_s.at[d], fp_r.at[d], p_dev)
+        send(where, fq_s.at[d], fq_r.at[d], q_dev)
+        send(where, fk_s.at[d], fk_r.at[d], k_dev)
+    for d in range(n_z):
+        where = place(r1, behind(d), y1, core)
+        receive(where, fp_s.at[d], fp_r.at[d], k_dev)
+        send(where, fq_s.at[n_z + d], fq_r.at[n_z + d], q_dev)
+        send(where, fk_s.at[n_z + d], fk_r.at[n_z + d], k_dev)
+    for side, (rr, yy) in enumerate(((r2, y2), (1 - r, 1 - y))):
+        for d in range(n_z):
+            where, at = place(rr, behind(d), yy, core), side * n_z + d
+            receive(where, fq_s.at[at], fq_r.at[at], k_dev)
+            send(where, fk_s.at[2 * n_z + at], fk_r.at[2 * n_z + at], k_dev)
+    for side, (rr, yy) in enumerate(((r, y), (r2, y2), (r1, y1), (1 - r, 1 - y))):
+        for d in range(n_z):
+            where, at = place(rr, behind(d), yy, 1 - core), side * n_z + d
+            receive(where, fk_s.at[at], fk_r.at[at], k_dev)
+
+    for copy in ended:
+        copy.wait_send()
+    for s in range(n_chip):
+        @pl.when(chip != s)
+        def _():
+            src = yown.at[s // halves, :, pl.ds((s % halves) * slab, slab)]
+            remote(src, slab_rows(c), a_s.at[s], a_r.at[chip], (r, 2 * s + core)).wait_send()
+    for needed, copy in late:
+        @pl.when(needed)
+        def _():
+            copy().wait_send()
+
+
+def one_kernel(inv_anc, factor_cols, couple, diag_inv, pattern, parent):
+    n_col = lax.axis_size("col")
+    count, rows, width = factor_cols.shape
+    npair = couple.shape[0]
+    n_z, n_chip = n_col // 4, n_col // 2
+    slab = count * width // n_chip
+    vmem, smem = pl.BlockSpec(memory_space=pltpu.VMEM), pl.BlockSpec(memory_space=pltpu.SMEM)
+    buffer = lambda *shape: pltpu.VMEM(shape, jnp.float32)
+    sems = lambda *shape: pltpu.SemaphoreType.DMA(shape)
+    twice = lambda *shape: [sems(*shape), sems(*shape)]
+    columns, window = pl.pallas_call(
+        functools.partial(window_kernel, n_col),
+        out_shape=(
+            jax.ShapeDtypeStruct((count, rows, width), jnp.float32),
+            jax.ShapeDtypeStruct((npair + count, width, width), jnp.float32),
+        ),
+        in_specs=[smem, smem, vmem, vmem, vmem, vmem],
+        out_specs=(vmem, vmem),
+        scratch_shapes=[
+            buffer(npair, width, width),
+            buffer(count, count, width, width),
+            buffer(count, n_col * rows, width),
+            buffer(count, 2, rows, width),
+            buffer(count, rows, width),
+            buffer(count, rows, width),
+            buffer(n_col * rows, slab),
+            buffer(3, slab, width),
+            buffer(slab, width),
+            *twice(count, n_z),
+            *twice(count, n_z),
+            *twice(count, 2 * n_z),
+            *twice(count),
+            *twice(n_chip),
+            *twice(n_chip),
+            pltpu.SemaphoreType.DMA,
+            pltpu.SemaphoreType.DMA,
+            *twice(n_z),
+            *twice(n_z),
+            *twice(2 * n_z),
+            *twice(4 * n_z),
+        ],
+        compiler_params=pltpu.CompilerParams(
+            collective_id=0, has_side_effects=True, vmem_limit_bytes=48 << 20
+        ),
+    )(pattern, parent, inv_anc.reshape(-1, rows, inv_anc.shape[3]), factor_cols, couple, diag_inv)
+    return columns, window[:npair], window[npair:]
+
+
 def solution(mesh):
     in_specs = (P(None, "col", None, "row"), P(None, ("row", "col"), None), P(), P(), P(), P())
     out_specs = (P(None, ("row", "col"), None), P(), P())
-    return jax.shard_map(shards, mesh=mesh, in_specs=in_specs, out_specs=out_specs, check_vma=False)
+
+    def body(inv_anc, factor_cols, couple, diag_inv, pattern, parent):
+        count, rows, width = factor_cols.shape
+        slab = count * width // (mesh.shape["col"] // 2)
+        fits = mesh.shape["row"] == 2 and mesh.shape["col"] == 4 * count
+        fits = fits and slab % 128 == 0 and rows % 16 == 0 and rows <= width and count == 4
+        run = one_kernel if fits else shards
+        return run(inv_anc, factor_cols, couple, diag_inv, pattern, parent)
+
+    return jax.shard_map(body, mesh=mesh, in_specs=in_specs, out_specs=out_specs, check_vma=False)

time: 202 us -> 79.5 us (0.39)
  the two profiles are of different devices: /device:TPU:0 before, /device:TPU:25 now
where the time goes in v2:
time: 79.5 us; the launch traced here: 79.2 us
  Pallas kernels  69.7 us (88%)
  local copies, waits for them, and re-layouts  8.89 us (11%)
    pallas_call x1, Pallas kernels, one_kernel(): pl.pallas_call(functools.partial(window_kernel, n_col), out_shape=(jax.Sh...  69.7 us
    unnamed x13, local copies, waits for them, and re-layouts  6.52 us
    slice x2, local copies, waits for them, and re-layouts, one_kernel(): return (columns, window[:npair], window[npair:])  2.37 us

profile of v2, /device:TPU:25, one launch (start us, length us, event | category | flops | bytes accessed | tf_op | source)
XLA Modules:
  0.0 79.2 jit_solution(18287520626658004820)
XLA Ops:
  0.6 0.0 copy-start
  0.6 1.4 %copy-done = f32[6,256,256]{2,1,0:T(8,128)S(1)} copy-done((f32[6,256,256]{2,1,0:T(8,128)S(1)}, f32[6,256,256]{2,1,0:T(8,128)}, u32[]{:S(2)}) %copy-start) | copy-done | bytes 1572888
  2.0 0.0 copy-start.1
  2.0 1.2 %copy-done.1 = f32[4,256,256]{2,1,0:T(8,128)S(1)} copy-done((f32[4,256,256]{2,1,0:T(8,128)S(1)}, f32[4,256,256]{2,1,0:T(8,128)}, u32[]{:S(2)}) %copy-start.1) | copy-done | bytes 1048600
  3.3 0.0 copy-start.2
  3.3 1.0 %copy-done.2 = f32[2,1,48,768]{3,2,1,0:T(8,128)S(1)} copy-done((f32[2,1,48,768]{3,2,1,0:T(8,128)S(1)}, f32[2,1,48,768]{3,2,1,0:T(8,128)}, u32[]{:S(2)}) %copy-start.2) | copy-done | bytes 294936
  4.2 0.0 copy-start.3
  4.2 0.9 %copy-done.3 = f32[4,48,256]{2,1,0:T(8,128)S(1)} copy-done((f32[4,48,256]{2,1,0:T(8,128)S(1)}, f32[4,48,256]{2,1,0:T(8,128)}, u32[]{:S(2)}) %copy-start.3) | copy-done | bytes 196632
  5.2 0.0 copy-start.4
  5.2 0.7 copy-done.4
  5.8 0.0 copy-start.5
  5.8 0.7 copy-done.5
  6.5 69.7 %shard_map.85 = (f32[4,48,256]{2,1,0:T(8,128)S(1)}, f32[10,256,256]{2,1,0:T(8,128)S(1)}) custom-call(s32[4,6]{1,0:T(4,128)S(1)} %copy-done.4, s32[4]{0:T(128)S(1)} %copy-done.5, f32[2,48,768]{2,1,0:T(8,128)S(1)} %bitcast.1, f32[4,48,256]{2,1,0:T(8,128)S(1)} %copy-done.3, f32[6,256,256]{2,1,0:T(8,128)S(1)} %copy-done, f32[4,256,256]{2,1,0:T(8,128)S(1)} %copy-done.1), custom_call_target="tpu_custom_call" | custom-call | tf_op jit(solution)/shard_map/pallas_call | solution.py:387
  76.2 1.0 %slice.7 = f32[4,256,256]{2,1,0:T(8,128)} slice(f32[10,256,256]{2,1,0:T(8,128)S(1)} %get-tuple-element.6), slice={[6:10], [0:256], [0:256]} | slice | bytes 2097152 | tf_op jit(solution)/shard_map/slice | solution.py:422
  77.2 1.3 %slice.6 = f32[6,256,256]{2,1,0:T(8,128)} slice(f32[10,256,256]{2,1,0:T(8,128)S(1)} %get-tuple-element.6), slice={[0:6], [0:256], [0:256]} | slice | bytes 3145728 | tf_op jit(solution)/shard_map/slice | solution.py:422
  78.6 0.7 copy.10
Async XLA Ops:
  0.6 1.4 %copy-start = (f32[6,256,256]{2,1,0:T(8,128)S(1)}, f32[6,256,256]{2,1,0:T(8,128)}, u32[]{:S(2)}) copy-start(f32[6,256,256]{2,1,0:T(8,128)} %couple.1) | copy-start | bytes 4718596
  2.0 1.2 %copy-start.1 = (f32[4,256,256]{2,1,0:T(8,128)S(1)}, f32[4,256,256]{2,1,0:T(8,128)}, u32[]{:S(2)}) copy-start(f32[4,256,256]{2,1,0:T(8,128)} %diag.1) | copy-start | bytes 3145732
  3.3 1.0 %copy-start.2 = (f32[2,1,48,768]{3,2,1,0:T(8,128)S(1)}, f32[2,1,48,768]{3,2,1,0:T(8,128)}, u32[]{:S(2)}) copy-start(f32[2,1,48,768]{3,2,1,0:T(8,128)} %param.6) | copy-start | bytes 884740
  4.2 0.9 %copy-start.3 = (f32[4,48,256]{2,1,0:T(8,128)S(1)}, f32[4,48,256]{2,1,0:T(8,128)}, u32[]{:S(2)}) copy-start(f32[4,48,256]{2,1,0:T(8,128)} %factor.1) | copy-start | bytes 589828
  5.2 0.7 copy-start.4
  5.8 0.7 copy-start.5

commit v3 on v2

--- a/solution.py
+++ b/solution.py
@@ -117,8 +117,8 @@
 
 
 def window_kernel(
-    n_col, pattern, parent, anc, factor, couple, diag, cols_out, win_out,
-    links, inverse, gath, ypart, xbuf, yown, ysl, gpart, gbuf,
+    n_col, pattern_in, parent_in, anc_in, factor_in, couple_in, diag_in, cols_out, win_out,
+    pattern, parent, anc, factor, couple, diag, in_s, links, inverse, gath, ypart, xbuf, yown, ysl, gpart, gbuf,
     z_s, z_r, y_s, y_r, k_s, k_r, x_s, x_r, a_s, a_r, b_s, b_r, g_s, g_r,
     fz_s, fz_r, fp_s, fp_r, fq_s, fq_r, fk_s, fk_r,
 ):
@@ -136,6 +136,22 @@
     def behind(d):
         return (z + n_z - d) % n_z
 
+    def slab_of(cc):
+        return (cc + n_chip - 2) % n_chip
+
+    mine_slab = slab_of(chip)
+
+    loads = [
+        pltpu.make_async_copy(src, dst, in_s.at[i])
+        for i, (src, dst) in enumerate(
+            (
+                (factor_in, factor), (pattern_in, pattern), (parent_in, parent),
+                (couple_in, couple), (diag_in, diag), (anc_in, anc),
+            )
+        )
+    ]
+    for load in loads:
+        load.start()
     barrier = pltpu.get_barrier_semaphore()
     for e in range(1, n_col):
         pl.semaphore_signal(barrier, inc=1, device_id=(r, (c + e) % n_col), device_id_type=MESH)
@@ -148,29 +164,40 @@
         )
 
     y_dev, k_dev, x_dev = (r, col_of(z, 1 - y, core)), (r, col_of(z, y, 1 - core)), (1 - r, c)
-    ended = []
+    late = []
 
     def begin(copy):
         copy.start()
-        ended.append(copy)
+        late.append((None, lambda: copy))
+
+    def later(needed, copy):
+        @pl.when(needed)
+        def _():
+            copy().start()
+
+        late.append((needed, copy))
 
     def slot(j, index):
         return gath.at[j, pl.ds(pl.multiple_of(index * rows, 16), rows), :]
 
-    linked = {}
-    for j in range(count):
-        for m in range(j):
-            now = parent[j] == m
-            for p in range(m + 1, j):
-                now = jnp.logical_or(now, jnp.logical_and(parent[j] == p, linked[p, m]))
-            linked[j, m] = now
-            pair = j * (j - 1) // 2 + m
-            links[pair] = couple[pair] * jnp.where(now, 1.0, 0.0)
     first_row = (r * n_col + c) * rows
     first_block, last_block = first_row // width, (first_row + rows - 1) // width
     inside = lax.broadcasted_iota(jnp.int32, (rows, width), 0) < (first_block + 1) * width - first_row
 
-    reduced = []
+    def along(j, step, d, index):
+        to = z - step
+        piece = lambda: slot(j, index)
+        side = (step + 1) // 2
+
+        def copy():
+            there = (r, col_of((to + n_z) % n_z, y, core))
+            return remote(piece(), piece(), z_s.at[j, side, d], z_r.at[j, side, d], there)
+
+        return jnp.logical_and(to >= 0, to < n_z), copy
+
+    reduced, coupled = [], {}
+    loads[0].wait()
+    loads[1].wait()
     for j in range(count):
         mask = jnp.where(
             inside,
@@ -179,17 +206,29 @@
         )
         current = factor[j] * mask
         for m in range(j):
-            current = current - dot3(reduced[m], split(links[j * (j - 1) // 2 + m]))
+            current = current - dot3(reduced[m], coupled[j, m])
         reduced.append(split(current))
         gath[j, pl.ds(pl.multiple_of(c * rows, 16), rows), :] = current
         if j == 0:
             pl.semaphore_wait(barrier, n_col)
         own = slot(j, c)
-        begin(remote(own, own, y_s.at[j, 0], y_r.at[j, 0], y_dev))
-        for d in range(1, n_z):
-            there = (r, col_of((z + d) % n_z, y, core))
-            begin(remote(own, own, z_s.at[j, d], z_r.at[j, d], there))
-        begin(remote(own, own, k_s.at[j, 0], k_r.at[j, 0], k_dev))
+        begin(remote(own, own, y_s.at[j, z], y_r.at[j, z], y_dev))
+        for step in (-1, 1):
+            later(*along(j, step, 1, c))
+        begin(remote(own, own, k_s.at[j, y * n_z + z], k_r.at[j, y * n_z + z], k_dev))
+        if j == 0:
+            loads[2].wait()
+            loads[3].wait()
+            linked = {}
+        if j + 1 < count:
+            for m in range(j + 1):
+                now = parent[j + 1] == m
+                for p in range(m + 1, j + 1):
+                    now = jnp.logical_or(now, jnp.logical_and(parent[j + 1] == p, linked[p, m]))
+                linked[j + 1, m] = now
+                pair = (j + 1) * j // 2 + m
+                links[pair] = couple[pair] * jnp.where(now, 1.0, 0.0)
+                coupled[j + 1, m] = split(links[pair])
 
     diagonal = (
         lax.broadcasted_iota(jnp.int32, (width, width), 0)
@@ -202,17 +241,38 @@
         for j in range(m + 1, count):
             total = links[j * (j - 1) // 2 + m]
             for q in range(m + 1, j):
-                total = total + dot3(split(inverse[m, q]), split(links[j * (j - 1) // 2 + q]))
+                total = total + dot3(split(inverse[m, q]), coupled[j, q])
             inverse[m, j] = -total
 
-    for j in range(count):
-        for d in range(1, n_z):
-            piece = slot(j, col_of(behind(d), y, core))
-            remote(piece, piece, z_s.at[j, d], z_r.at[j, d], y_dev).wait_recv()
-            begin(remote(piece, piece, y_s.at[j, d], y_r.at[j, d], y_dev))
-            begin(remote(piece, piece, k_s.at[j, d], k_r.at[j, d], k_dev))
-
-    m, h = chip // halves, chip % halves
+    for d in range(1, n_z):
+        for j in range(count):
+            for step in (-1, 1):
+                source = z + step * d
+                from_z = (source + n_z) % n_z
+                index = col_of(from_z, y, core)
+                side = (step + 1) // 2
+                there = jnp.logical_and(source >= 0, source < n_z)
+
+                def to_y(j=j, index=index, from_z=from_z):
+                    piece = slot(j, index)
+                    return remote(piece, piece, y_s.at[j, from_z], y_r.at[j, from_z], y_dev)
+
+                def to_core(j=j, index=index, from_z=from_z):
+                    piece, at = slot(j, index), y * n_z + from_z
+                    return remote(piece, piece, k_s.at[j, at], k_r.at[j, at], k_dev)
+
+                @pl.when(there)
+                def _():
+                    piece = slot(j, index)
+                    remote(piece, piece, z_s.at[j, side, d], z_r.at[j, side, d], k_dev).wait_recv()
+
+                if d + 1 < n_z:
+                    further, onward = along(j, step, d + 1, index)
+                    later(jnp.logical_and(there, further), onward)
+                later(there, to_y)
+                later(there, to_core)
+
+    m, h = mine_slab // halves, mine_slab % halves
 
     def q_of(rr):
         rho = (rr + z) % 2
@@ -222,25 +282,27 @@
     j_own, j_other = jnp.minimum(m + q_own, count - 1), jnp.minimum(m + q_other, count - 1)
     half = pl.ds(pl.multiple_of(h * slab, slab), slab)
     piece_sum = jnp.zeros((slab, width), jnp.float32)
+    loads[4].wait()
     for q in range(count):
         left = inverse[q, m, :, half].T
         middle = dot3(split(left), split(diag[q]))
         piece_sum = piece_sum + dot3(split(middle), split(inverse[q, j_own]))
     gpart[2] = piece_sum
 
+    loads[5].wait()
     left_anc = split(anc[...].reshape(2 * rows, anc.shape[2]))
 
     def relay(j):
         for d in range(n_z):
-            piece = slot(j, col_of(behind(d), 1 - y, core))
-            remote(piece, piece, y_s.at[j, d], y_r.at[j, d], y_dev).wait_recv()
-            begin(remote(piece, piece, k_s.at[j, n_z + d], k_r.at[j, n_z + d], k_dev))
+            from_z = behind(d)
+            piece, at = slot(j, col_of(from_z, 1 - y, core)), (1 - y) * n_z + from_z
+            remote(piece, piece, y_s.at[j, from_z], y_r.at[j, from_z], y_dev).wait_recv()
+            begin(remote(piece, piece, k_s.at[j, at], k_r.at[j, at], k_dev))
 
     def multiply(j):
-        for d in range(n_z):
-            for side, yy in ((0, y), (1, 1 - y)):
-                piece = slot(j, col_of(behind(d), yy, 1 - core))
-                at = side * n_z + d
+        for yy in range(2):
+            for zz in range(n_z):
+                piece, at = slot(j, col_of(zz, yy, 1 - core)), yy * n_z + zz
                 remote(piece, piece, k_s.at[j, at], k_r.at[j, at], k_dev).wait_recv()
         ypart[j] = dot3(left_anc, split(gath[j])).reshape(2, rows, width)
         begin(remote(ypart.at[j, 1 - r], xbuf.at[j], x_s.at[j], x_r.at[j], x_dev))
@@ -252,16 +314,17 @@
         cols_out[j] = -total
         for part in range(halves):
             s = j * halves + part
+            target = (s + 2) % n_chip
             src = yown.at[j, :, pl.ds(part * slab, slab)]
             dst = ysl.at[pl.ds(pl.multiple_of(c * rows, 16), rows), :]
 
-            @pl.when(chip == s)
+            @pl.when(chip == target)
             def _():
                 ysl[pl.ds(pl.multiple_of(c * rows, 16), rows), :] = total[:, part * slab : (part + 1) * slab]
 
-            @pl.when(chip != s)
+            @pl.when(chip != target)
             def _():
-                remote(src, dst, a_s.at[s], a_r.at[chip], (r, 2 * s + core)).start()
+                remote(src, dst, a_s.at[s], a_r.at[chip], (r, 2 * target + core)).start()
 
     for j in range(count):
         relay(j)
@@ -295,7 +358,7 @@
     def place(rr, zz, yy, kk):
         rho = (rr + zz) % 2
         q = (1 - kk) * 3 * rho + kk * (2 - rho)
-        block, part = (2 * zz + yy) // halves, (2 * zz + yy) % halves
+        block, part = slab_of(2 * zz + yy) // halves, slab_of(2 * zz + yy) % halves
         j = block + q
         off = (q + 3) // 4
         index = off * (j * (j - 1) // 2 + block) + (1 - off) * (npair + block)
@@ -309,15 +372,6 @@
     r1, y1 = r + core * flip_x, y + (1 - core) * flip_y
     r2, y2 = r + (1 - core) * flip_x, y + core * flip_y
     p_dev, q_dev = (r1, col_of(z, y1, core)), (r2, col_of(z, y2, core))
-    late = []
-
-    def later(needed, copy):
-        @pl.when(needed)
-        def _():
-            copy().start()
-
-        late.append((needed, copy))
-
     def send(where, send_sem, recv_sem, device):
         def copy():
             piece = at_piece(where)
@@ -361,17 +415,29 @@
             where, at = place(rr, behind(d), yy, 1 - core), side * n_z + d
             receive(where, fk_s.at[at], fk_r.at[at], k_dev)
 
-    for copy in ended:
-        copy.wait_send()
     for s in range(n_chip):
-        @pl.when(chip != s)
+        target = (s + 2) % n_chip
+
+        @pl.when(chip != target)
         def _():
             src = yown.at[s // halves, :, pl.ds((s % halves) * slab, slab)]
-            remote(src, slab_rows(c), a_s.at[s], a_r.at[chip], (r, 2 * s + core)).wait_send()
+            remote(src, slab_rows(c), a_s.at[s], a_r.at[chip], (r, 2 * target + core)).wait_send()
     for needed, copy in late:
-        @pl.when(needed)
-        def _():
+        if needed is None:
             copy().wait_send()
+        else:
+            @pl.when(needed)
+            def _():
+                copy().wait_send()
+
+
+def deliver(npair, columns, window, cols_out, pairs_out, diag_out, done):
+    parts = ((window.at[:npair], pairs_out), (window.at[npair:], diag_out), (columns, cols_out))
+    copies = [pltpu.make_async_copy(src, dst, done.at[i]) for i, (src, dst) in enumerate(parts)]
+    for copy in copies:
+        copy.start()
+    for copy in copies:
+        copy.wait()
 
 
 def one_kernel(inv_anc, factor_cols, couple, diag_inv, pattern, parent):
@@ -380,7 +446,9 @@
     npair = couple.shape[0]
     n_z, n_chip = n_col // 4, n_col // 2
     slab = count * width // n_chip
-    vmem, smem = pl.BlockSpec(memory_space=pltpu.VMEM), pl.BlockSpec(memory_space=pltpu.SMEM)
+    vmem, hbm = pl.BlockSpec(memory_space=pltpu.VMEM), pl.BlockSpec(memory_space=pltpu.HBM)
+    anywhere = pl.BlockSpec(memory_space=pl.ANY)
+    anc = inv_anc.reshape(-1, rows, inv_anc.shape[3])
     buffer = lambda *shape: pltpu.VMEM(shape, jnp.float32)
     sems = lambda *shape: pltpu.SemaphoreType.DMA(shape)
     twice = lambda *shape: [sems(*shape), sems(*shape)]
@@ -390,9 +458,16 @@
             jax.ShapeDtypeStruct((count, rows, width), jnp.float32),
             jax.ShapeDtypeStruct((npair + count, width, width), jnp.float32),
         ),
-        in_specs=[smem, smem, vmem, vmem, vmem, vmem],
+        in_specs=[hbm] * 6,
         out_specs=(vmem, vmem),
         scratch_shapes=[
+            pltpu.SMEM(pattern.shape, jnp.int32),
+            pltpu.SMEM(parent.shape, jnp.int32),
+            buffer(*anc.shape),
+            buffer(*factor_cols.shape),
+            buffer(*couple.shape),
+            buffer(*diag_inv.shape),
+            sems(6),
             buffer(npair, width, width),
             buffer(count, count, width, width),
             buffer(count, n_col * rows, width),
@@ -402,7 +477,7 @@
             buffer(n_col * rows, slab),
             buffer(3, slab, width),
             buffer(slab, width),
-            *twice(count, n_z),
+            *twice(count, 2, n_z),
             *twice(count, n_z),
             *twice(count, 2 * n_z),
             *twice(count),
@@ -416,10 +491,19 @@
             *twice(4 * n_z),
         ],
         compiler_params=pltpu.CompilerParams(
-            collective_id=0, has_side_effects=True, vmem_limit_bytes=48 << 20
+            collective_id=0, has_side_effects=True, vmem_limit_bytes=63 << 20
         ),
-    )(pattern, parent, inv_anc.reshape(-1, rows, inv_anc.shape[3]), factor_cols, couple, diag_inv)
-    return columns, window[:npair], window[npair:]
+    )(pattern, parent, anc, factor_cols, couple, diag_inv)
+    return pl.pallas_call(
+        functools.partial(deliver, npair),
+        out_shape=tuple(
+            jax.ShapeDtypeStruct(like.shape, jnp.float32) for like in (factor_cols, couple, diag_inv)
+        ),
+        in_specs=[anywhere] * 2,
+        out_specs=(anywhere,) * 3,
+        scratch_shapes=[sems(3)],
+        compiler_params=pltpu.CompilerParams(vmem_limit_bytes=63 << 20),
+    )(columns, window)
 
 
 def solution(mesh):

time: 79.5 us -> 150 us (1.89)
  the two profiles are of different devices: /device:TPU:25 before, /device:TPU:0 now
where the time goes in v3:
time: 150 us; the launch traced here: 149 us
  Pallas kernels  148 us (99%)
    pallas_call x1, Pallas kernels, one_kernel(): pl.pallas_call(functools.partial(deliver, npair), out_shape=tuple((jax.Sh...  86.5 us
    pallas_call x1, Pallas kernels, one_kernel(): pl.pallas_call(functools.partial(window_kernel, n_col), out_shape=(jax.Sh...  61.8 us

profile of v3, /device:TPU:0, one launch (start us, length us, event | category | flops | bytes accessed | tf_op | source)
XLA Modules:
  0.0 149.0 jit_solution(2364396899907062334)
XLA Ops:
  0.6 61.8 %shard_map.85 = (f32[4,48,256]{2,1,0:T(8,128)}, f32[10,256,256]{2,1,0:T(8,128)}) custom-call(s32[4,6]{1,0:T(4,128)} %pattern_in.1, s32[4]{0:T(128)} %parent_in.1, f32[2,48,768]{2,1,0:T(8,128)} %bitcast.1, f32[4,48,256]{2,1,0:T(8,128)} %factor_in.1, f32[6,256,256]{2,1,0:T(8,128)} %couple_in.1, f32[4,256,256]{2,1,0:T(8,128)} %diag_in.1), custom_call_target="tpu_custom_call" | custom-call | tf_op jit(solution)/shard_map/pallas_call | solution.py:455
  62.5 86.5 %shard_map.86 = (f32[4,48,256]{2,1,0:T(8,128)}, f32[6,256,256]{2,1,0:T(8,128)}, f32[4,256,256]{2,1,0:T(8,128)}) custom-call(f32[4,48,256]{2,1,0:T(8,128)} %get-tuple-element.5.columns, f32[10,256,256]{2,1,0:T(8,128)} %get-tuple-element.6.window), custom_call_target="tpu_custom_call" | custom-call | tf_op jit(solution)/shard_map/pallas_call | solution.py:497

commit v4 on v3

--- a/solution.py
+++ b/solution.py
@@ -431,15 +431,6 @@
                 copy().wait_send()
 
 
-def deliver(npair, columns, window, cols_out, pairs_out, diag_out, done):
-    parts = ((window.at[:npair], pairs_out), (window.at[npair:], diag_out), (columns, cols_out))
-    copies = [pltpu.make_async_copy(src, dst, done.at[i]) for i, (src, dst) in enumerate(parts)]
-    for copy in copies:
-        copy.start()
-    for copy in copies:
-        copy.wait()
-
-
 def one_kernel(inv_anc, factor_cols, couple, diag_inv, pattern, parent):
     n_col = lax.axis_size("col")
     count, rows, width = factor_cols.shape
@@ -447,7 +438,6 @@
     n_z, n_chip = n_col // 4, n_col // 2
     slab = count * width // n_chip
     vmem, hbm = pl.BlockSpec(memory_space=pltpu.VMEM), pl.BlockSpec(memory_space=pltpu.HBM)
-    anywhere = pl.BlockSpec(memory_space=pl.ANY)
     anc = inv_anc.reshape(-1, rows, inv_anc.shape[3])
     buffer = lambda *shape: pltpu.VMEM(shape, jnp.float32)
     sems = lambda *shape: pltpu.SemaphoreType.DMA(shape)
@@ -494,16 +484,7 @@
             collective_id=0, has_side_effects=True, vmem_limit_bytes=63 << 20
         ),
     )(pattern, parent, anc, factor_cols, couple, diag_inv)
-    return pl.pallas_call(
-        functools.partial(deliver, npair),
-        out_shape=tuple(
-            jax.ShapeDtypeStruct(like.shape, jnp.float32) for like in (factor_cols, couple, diag_inv)
-        ),
-        in_specs=[anywhere] * 2,
-        out_specs=(anywhere,) * 3,
-        scratch_shapes=[sems(3)],
-        compiler_params=pltpu.CompilerParams(vmem_limit_bytes=63 << 20),
-    )(columns, window)
+    return columns, window[:npair], window[npair:]
 
 
 def solution(mesh):

time: 150 us -> 68.8 us (0.46)
  Pallas kernels: 148 us -> 61.8 us
  local copies, waits for them, and re-layouts: 0 us -> 5.74 us
    pallas_call x1 -> x0, Pallas kernels: 86.5 us -> none  [one_kernel(): pl.pallas_call(functools.partial(deliver, npair), out_shape=tuple((jax.Sh...]
    slice x0 -> x2, local copies, waits for them, and re-layouts: none -> 5.06 us  [one_kernel(): return (columns, window[:npair], window[npair:])]
where the time goes in v4:
time: 68.8 us; the launch traced here: 68.2 us
  Pallas kernels  61.8 us (90%)
  local copies, waits for them, and re-layouts  5.74 us (8%)
    pallas_call x1, Pallas kernels, one_kernel(): pl.pallas_call(functools.partial(window_kernel, n_col), out_shape=(jax.Sh...  61.8 us
    slice x2, local copies, waits for them, and re-layouts, one_kernel(): return (columns, window[:npair], window[npair:])  5.06 us

profile of v4, /device:TPU:0, one launch (start us, length us, event | category | flops | bytes accessed | tf_op | source)
XLA Modules:
  0.0 68.2 jit_solution(15758439364162382305)
XLA Ops:
  0.6 61.8 %shard_map.85 = (f32[4,48,256]{2,1,0:T(8,128)}, f32[10,256,256]{2,1,0:T(8,128)}) custom-call(s32[4,6]{1,0:T(4,128)} %pattern_in.1, s32[4]{0:T(128)} %parent_in.1, f32[2,48,768]{2,1,0:T(8,128)} %bitcast.1, f32[4,48,256]{2,1,0:T(8,128)} %factor_in.1, f32[6,256,256]{2,1,0:T(8,128)} %couple_in.1, f32[4,256,256]{2,1,0:T(8,128)} %diag_in.1), custom_call_target="tpu_custom_call" | custom-call | tf_op jit(solution)/shard_map/pallas_call | solution.py:445
  62.5 2.3 %slice.7 = f32[4,256,256]{2,1,0:T(8,128)} slice(f32[10,256,256]{2,1,0:T(8,128)} %get-tuple-element.6), slice={[6:10], [0:256], [0:256]} | slice | bytes 2097152 | tf_op jit(solution)/shard_map/slice | solution.py:487
  64.8 0.0 copy-start
  64.8 2.8 %slice.6 = f32[6,256,256]{2,1,0:T(8,128)} slice(f32[10,256,256]{2,1,0:T(8,128)} %get-tuple-element.6), slice={[0:6], [0:256], [0:256]} | slice | bytes 3145728 | tf_op jit(solution)/shard_map/slice | solution.py:487
  67.5 0.0 copy-done
  67.5 0.7 copy.10
Async XLA Ops:
  64.8 2.8 %copy-start = (f32[4,48,256]{2,1,0:T(8,128)S(1)}, f32[4,48,256]{2,1,0:T(8,128)}, u32[]{:S(2)}) copy-start(f32[4,48,256]{2,1,0:T(8,128)} %get-tuple-element.10) | copy-start | bytes 589828

commit v5 on v4

--- a/solution.py
+++ b/solution.py
@@ -230,6 +230,34 @@
                 links[pair] = couple[pair] * jnp.where(now, 1.0, 0.0)
                 coupled[j + 1, m] = split(links[pair])
 
+    for d in range(1, n_z):
+        for j in range(count):
+            for step in (-1, 1):
+                source = z + step * d
+                from_z = (source + n_z) % n_z
+                index = col_of(from_z, y, core)
+                side = (step + 1) // 2
+                there = jnp.logical_and(source >= 0, source < n_z)
+
+                def to_y(j=j, index=index, from_z=from_z):
+                    piece = slot(j, index)
+                    return remote(piece, piece, y_s.at[j, from_z], y_r.at[j, from_z], y_dev)
+
+                def to_core(j=j, index=index, from_z=from_z):
+                    piece, at = slot(j, index), y * n_z + from_z
+                    return remote(piece, piece, k_s.at[j, at], k_r.at[j, at], k_dev)
+
+                @pl.when(there)
+                def _():
+                    piece = slot(j, index)
+                    remote(piece, piece, z_s.at[j, side, d], z_r.at[j, side, d], k_dev).wait_recv()
+
+                later(there, to_y)
+                if d + 1 < n_z:
+                    further, onward = along(j, step, d + 1, index)
+                    later(jnp.logical_and(there, further), onward)
+                later(there, to_core)
+
     diagonal = (
         lax.broadcasted_iota(jnp.int32, (width, width), 0)
         == lax.broadcasted_iota(jnp.int32, (width, width), 1)
@@ -243,34 +271,6 @@
             for q in range(m + 1, j):
                 total = total + dot3(split(inverse[m, q]), coupled[j, q])
             inverse[m, j] = -total
-
-    for d in range(1, n_z):
-        for j in range(count):
-            for step in (-1, 1):
-                source = z + step * d
-                from_z = (source + n_z) % n_z
-                index = col_of(from_z, y, core)
-                side = (step + 1) // 2
-                there = jnp.logical_and(source >= 0, source < n_z)
-
-                def to_y(j=j, index=index, from_z=from_z):
-                    piece = slot(j, index)
-                    return remote(piece, piece, y_s.at[j, from_z], y_r.at[j, from_z], y_dev)
-
-                def to_core(j=j, index=index, from_z=from_z):
-                    piece, at = slot(j, index), y * n_z + from_z
-                    return remote(piece, piece, k_s.at[j, at], k_r.at[j, at], k_dev)
-
-                @pl.when(there)
-                def _():
-                    piece = slot(j, index)
-                    remote(piece, piece, z_s.at[j, side, d], z_r.at[j, side, d], k_dev).wait_recv()
-
-                if d + 1 < n_z:
-                    further, onward = along(j, step, d + 1, index)
-                    later(jnp.logical_and(there, further), onward)
-                later(there, to_y)
-                later(there, to_core)
 
     m, h = mine_slab // halves, mine_slab % halves
 

time: 68.8 us -> 69.1 us (level)
  no operation moved by 1% of the time
where the time goes in v5:
time: 69.1 us; the launch traced here: 68.2 us
  Pallas kernels  61.8 us (89%)
  local copies, waits for them, and re-layouts  5.74 us (8%)
    pallas_call x1, Pallas kernels, one_kernel(): pl.pallas_call(functools.partial(window_kernel, n_col), out_shape=(jax.Sh...  61.8 us
    slice x2, local copies, waits for them, and re-layouts, one_kernel(): return (columns, window[:npair], window[npair:])  5.06 us

profile of v5, /device:TPU:0, one launch (start us, length us, event | category | flops | bytes accessed | tf_op | source)
XLA Modules:
  0.0 68.2 jit_solution(10696770755071796968)
XLA Ops:
  0.6 61.8 %shard_map.85 = (f32[4,48,256]{2,1,0:T(8,128)}, f32[10,256,256]{2,1,0:T(8,128)}) custom-call(s32[4,6]{1,0:T(4,128)} %pattern_in.1, s32[4]{0:T(128)} %parent_in.1, f32[2,48,768]{2,1,0:T(8,128)} %bitcast.1, f32[4,48,256]{2,1,0:T(8,128)} %factor_in.1, f32[6,256,256]{2,1,0:T(8,128)} %couple_in.1, f32[4,256,256]{2,1,0:T(8,128)} %diag_in.1), custom_call_target="tpu_custom_call" | custom-call | tf_op jit(solution)/shard_map/pallas_call | solution.py:445
  62.5 2.3 %slice.7 = f32[4,256,256]{2,1,0:T(8,128)} slice(f32[10,256,256]{2,1,0:T(8,128)} %get-tuple-element.6), slice={[6:10], [0:256], [0:256]} | slice | bytes 2097152 | tf_op jit(solution)/shard_map/slice | solution.py:487
  64.8 0.0 copy-start
  64.8 2.8 %slice.6 = f32[6,256,256]{2,1,0:T(8,128)} slice(f32[10,256,256]{2,1,0:T(8,128)} %get-tuple-element.6), slice={[0:6], [0:256], [0:256]} | slice | bytes 3145728 | tf_op jit(solution)/shard_map/slice | solution.py:487
  67.5 0.0 copy-done
  67.5 0.7 copy.10
Async XLA Ops:
  64.8 2.8 %copy-start = (f32[4,48,256]{2,1,0:T(8,128)S(1)}, f32[4,48,256]{2,1,0:T(8,128)}, u32[]{:S(2)}) copy-start(f32[4,48,256]{2,1,0:T(8,128)} %get-tuple-element.10) | copy-start | bytes 589828
